TPU v7x, 32 devices: a whole 2x2x4 slice. The times are simulated.
32 devices in a mesh: seq: 8 (over z, x), fsdp: 4 (over y, core).
Axes of the slice: x: 2, y: 2, z: 4, core: 2. Of those that a mesh axis runs over, the one named last changes fastest.
Arguments:
- projected: bfloat16 [64, 65536], P('seq'), may hold values from -70 to 70
- cached: bfloat16 [128, 320, 7168], P('seq', None, 'fsdp'), may hold values from -6 to 6
- stream: bfloat16 [64, 7168], P('seq'), may hold values from -700 to 700
- norm_gain: float32 [7168], replicated, may hold values from 0.5 to 2
- routes: int32 [64, 8], P('seq'), may hold values from 0 to 255, as said below
- route_gates: float32 [64, 8], P('seq'), may hold values from 0.2 to 1
- gate_weight: bfloat16 [7168, 16384], P('fsdp', 'seq'), may hold values from -0.0625 to 0.0625
- up_weight: bfloat16 [7168, 16384], P('fsdp', 'seq'), may hold values from -0.0625 to 0.0625
- down_weight: bfloat16 [16384, 7168], P('seq', 'fsdp'), may hold values from -0.125 to 0.125
Outputs:
- attention: bfloat16 [64, 16384], P('seq')
- routed: bfloat16 [64, 7168], P('seq', 'fsdp')
Inputs may be any that keep to these rules, and one draw needn't show every extreme that they name: `routes`: each row names 8 different experts. Within the 8 rows of one device, at most 2 rows name any one expert below 8, and in every such block some expert below 8 is named by exactly 2 rows.
All inputs are finite; a program needn't handle non-finite values.
Results may differ from a plain program's by a relative error of at most 0.0071.
Values may be sent and summed in bfloat16 or wider, within the bound.
A program may use at most 192 MiB of HBM per device.

v0:
```python
import math

import jax
import jax.numpy as jnp
from jax import lax
from jax.sharding import PartitionSpec as P

QK_DIM = 192
V_DIM = 128
WAVE_EXPERTS = 8
CAPACITY = 2


def on_device(
    projected, cached, stream, norm_gain, routes, route_gates, gate_weight, up_weight, down_weight
):
    shard_set = (gate_weight, up_weight)
    pack_width = 2 * QK_DIM + V_DIM
    heads_here = cached.shape[0]
    cache_len = cached.shape[2]
    gathered = lax.all_to_all(projected, "seq", split_axis=1, concat_axis=0, tiled=True)
    span_len = gathered.shape[0]
    heads_major = jnp.transpose(gathered.reshape(span_len, heads_here, pack_width), (1, 0, 2))
    quarter = span_len // lax.axis_size("fsdp")
    first_key = lax.axis_index("fsdp") * quarter
    rows_block = math.gcd(512, span_len)
    block_count = span_len // rows_block
    score_scale = 1.0 / math.sqrt(QK_DIM)
    contract = (((1,), (1,)), ((), ()))

    def head_scores(head_pair):
        stacked, stored = head_pair
        key_rows = lax.dynamic_slice_in_dim(stacked[:, QK_DIM : 2 * QK_DIM], first_key, quarter, 0)
        query_blocks = stacked[:, :QK_DIM].reshape(block_count, rows_block, QK_DIM)

        def one_block(queries):
            span_scores = (
                lax.dot_general(queries, key_rows, contract, preferred_element_type=jnp.float32)
                * score_scale
            )
            cache_scores = (
                jnp.dot(queries, stored[:QK_DIM], preferred_element_type=jnp.float32) * score_scale
            )
            return jnp.concatenate([span_scores, cache_scores], axis=1)

        return lax.map(one_block, query_blocks).reshape(span_len, quarter + cache_len)

    scores = lax.map(head_scores, (heads_major, cached))
    query_pos = jnp.arange(span_len, dtype=jnp.int32)
    key_pos = first_key + jnp.arange(quarter, dtype=jnp.int32)
    span_open = key_pos[None, :] <= query_pos[:, None]
    open_mask = jnp.concatenate([span_open, jnp.ones((span_len, cache_len), bool)], axis=1)
    scores = jnp.where(open_mask[None], scores, -jnp.inf)
    highest = lax.pmax(jnp.max(scores, axis=2), "fsdp")
    exp_weights = jnp.where(open_mask[None], jnp.exp(scores - highest[:, :, None]), 0.0)
    key_total = jnp.sum(exp_weights, axis=2)
    weights_bf = exp_weights.astype(jnp.bfloat16)

    def head_values(head_item):
        weights_row, stacked, stored = head_item
        value_rows = lax.dynamic_slice_in_dim(stacked[:, 2 * QK_DIM :], first_key, quarter, 0)
        span_part = jnp.dot(
            weights_row[:, :quarter], value_rows, preferred_element_type=jnp.float32
        )
        cache_part = lax.dot_general(
            weights_row[:, quarter:], stored[QK_DIM:], contract, preferred_element_type=jnp.float32
        )
        return span_part + cache_part

    weighted = lax.map(head_values, (weights_bf, heads_major, cached))
    weighted, key_total = lax.psum((weighted, key_total), "fsdp")
    outputs = (weighted / key_total[:, :, None]).astype(jnp.bfloat16)
    merged = jnp.transpose(outputs, (1, 0, 2)).reshape(span_len, heads_here * V_DIM)
    attention = lax.all_to_all(merged, "seq", split_axis=0, concat_axis=1, tiled=True)
    tokens = stream.astype(jnp.float32)
    tok_count = tokens.shape[0]
    width_full = tokens.shape[1]
    slice_cols = gate_weight.shape[0]
    normed = (
        tokens * lax.rsqrt(jnp.mean(tokens * tokens, axis=1, keepdims=True) + 1e-06) * norm_gain
    ).astype(jnp.bfloat16)
    experts_here = jnp.arange(WAVE_EXPERTS, dtype=jnp.int32)
    matches = routes[:, :, None] == experts_here[None, None, :]
    hit_counts = jnp.sum(matches.astype(jnp.int32), axis=1)
    weight_of = jnp.sum(jnp.where(matches, route_gates[:, :, None], 0.0), axis=1)
    rank_rows = jnp.cumsum(hit_counts, axis=0) - 1
    slot_ids = jnp.arange(CAPACITY, dtype=jnp.int32)
    placed = (hit_counts[None, :, :] == 1) & (rank_rows[None, :, :] == slot_ids[:, None, None])
    placed = jnp.transpose(placed, (2, 0, 1)).astype(jnp.float32)
    slot_weight = jnp.einsum("ect,te->ec", placed, weight_of, precision=lax.Precision.HIGHEST)
    placed_flat = placed.reshape(WAVE_EXPERTS * CAPACITY, tok_count)
    send_rows = jnp.dot(
        placed_flat.astype(jnp.bfloat16), normed, preferred_element_type=jnp.float32
    ).astype(jnp.bfloat16)
    group_size = lax.axis_size("seq") // WAVE_EXPERTS
    outgoing = jnp.broadcast_to(
        send_rows.reshape(WAVE_EXPERTS, 1, CAPACITY, width_full),
        (WAVE_EXPERTS, group_size, CAPACITY, width_full),
    )
    outgoing = outgoing.reshape(WAVE_EXPERTS * group_size, CAPACITY, width_full)
    shard_set = (
        lax.all_gather(gate_weight, "fsdp", axis=0, tiled=True),
        lax.all_gather(up_weight, "fsdp", axis=0, tiled=True),
    )
    received = lax.all_to_all(outgoing, "seq", split_axis=0, concat_axis=0, tiled=True)
    rows_in = received.reshape(-1, received.shape[2])
    full_gate, full_up = shard_set
    gate_act = jnp.dot(rows_in, full_gate, preferred_element_type=jnp.float32)
    upward = jnp.dot(rows_in, full_up, preferred_element_type=jnp.float32)
    hidden = (jax.nn.silu(gate_act) * upward).astype(jnp.bfloat16)
    partial_value = jnp.dot(hidden, down_weight, preferred_element_type=jnp.float32).astype(
        jnp.bfloat16
    )
    partial_value = partial_value.reshape(received.shape[0], received.shape[1], slice_cols)
    result = lax.all_to_all(partial_value, "seq", split_axis=0, concat_axis=0, tiled=True)
    expert_out = jnp.sum(
        result.reshape(WAVE_EXPERTS, group_size, CAPACITY, slice_cols).astype(jnp.float32), axis=1
    )
    weighted_out = expert_out * slot_weight[:, :, None]
    mixed_rows = lax.dot_general(
        placed_flat,
        weighted_out.reshape(WAVE_EXPERTS * CAPACITY, slice_cols),
        (((0,), (0,)), ((), ())),
        precision=lax.Precision.HIGHEST,
    )
    routed = mixed_rows.astype(jnp.bfloat16)
    return (attention, routed)


def solution(mesh):
    placed = (
        P("seq", None),
        P("seq", None, "fsdp"),
        P("seq", None),
        P(),
        P("seq", None),
        P("seq", None),
        P("fsdp", "seq"),
        P("fsdp", "seq"),
        P("seq", "fsdp"),
    )
    return jax.shard_map(
        on_device,
        mesh=mesh,
        in_specs=placed,
        out_specs=(P("seq", None), P("seq", "fsdp")),
        check_vma=False,
    )
```

profile of v0, /device:TPU:0, one launch (start us, length us, event | category | flops | bytes accessed | tf_op | source)
XLA Modules:
  0.0 575.3 jit_solution(17097472984332643926)
XLA Ops:
  7.2 7.3 %all-to-all-start = ((bf16[8,8,8192]{2,0,1:T(8,128)(2,1)}), bf16[8,8,8192]{2,0,1:T(8,128)(2,1)S(1)}, u32[]{:S(2)}, u32[]{:S(2)}) async-start(bf16[8,8,8192]{2,0,1:T(8,128)(2,1)} %bitcast.74), calls=%async_computation | async-start | bytes 2097152 | tf_op jit(solution)/shard_map/all_to_all | solution.py:21
  14.6 25.6 %all-to-all-done = bf16[8,8,8192]{2,0,1:T(8,128)(2,1)S(1)} async-done(((bf16[8,8,8192]{2,0,1:T(8,128)(2,1)}), bf16[8,8,8192]{2,0,1:T(8,128)(2,1)S(1)}, u32[]{:S(2)}, u32[]{:S(2)}) %all-to-all-start) | async-done | bytes 1048608 | tf_op jit(solution)/shard_map/all_to_all | solution.py:21
  41.1 42.4 %while.30 = (s32[]{:T(128)}, f32[16,64,1808]{2,1,0:T(8,128)}, bf16[16,64,512]{2,1,0:T(8,128)(2,1)S(1)}, s32[]{:T(128)}, bf16[16,320,1792]{2,1,0:T(8,128)(2,1)}) while((s32[]{:T(128)}, f32[16,64,1808]{2,1,0:T(8,128)}, bf16[16,64,512]{2,1,0:T(8,128)(2,1)S(1)}, s32[]{:T(128)}, bf16[16,320,1792]{2,1,0:T(8,128)(2,1)}) %tuple.67), condition=%wide.region_1.2_spmd.clone, body=%wide.region_0.1_spmd.sunk.clone | while | flops 44664832 | bytes 2368581 | solution.py:48
  83.5 4.1 select_reduce_fusion
  87.6 5.8 %pmax.7 = f32[16,64]{1,0:T(8,128)S(1)} all-reduce(f32[16,64]{1,0:T(8,128)S(1)} %select_reduce_fusion), channel_id=1, replica_groups=mesh['seq'=8,'fsdp'=4] {'fsdp'}, use_global_device_ids=true, to_apply=%region_3.4 | all-reduce | flops 1024 | bytes 8192 | tf_op jit(solution)/shard_map/pmax | solution.py:54
  93.4 5.7 fusion.14
  99.1 49.2 %while.31 = (s32[]{:T(128)}, f32[16,64,128]{2,1,0:T(8,128)}, bf16[16,64,1808]{2,1,0:T(8,128)(2,1)}, bf16[16,64,512]{2,1,0:T(8,128)(2,1)S(1)}, s32[]{:T(128)}, /*index=5*/bf16[16,320,1792]{2,1,0:T(8,128)(2,1)}) while((s32[]{:T(128)}, f32[16,64,128]{2,1,0:T(8,128)}, bf16[16,64,1808]{2,1,0:T(8,128)(2,1)}, ...), condition=%wide.region_5.6_spmd.clone, body=%wide.region_4.5_spmd.sunk.clone | while | flops 29630468 | bytes 1434721 | solution.py:70
  103.3 2.0 fusion.73
  109.4 2.0 fusion.73
  115.6 2.0 fusion.73
  121.7 2.0 fusion.73
  127.9 2.0 fusion.73
  140.2 2.0 fusion.73
  151.5 4.8 all-to-all-start.2
  156.5 7.8 %all-to-all-done.2 = bf16[8,2,7168]{2,1,0:T(2,128)(2,1)S(1)} async-done(((bf16[8,2,7168]{2,1,0:T(2,128)(2,1)}), bf16[8,2,7168]{2,1,0:T(2,128)(2,1)S(1)}, u32[]{:S(2)}, u32[]{:S(2)}) %all-to-all-start.2) | async-done | bytes 229408 | tf_op jit(solution)/shard_map/all_to_all | solution.py:105
  164.4 5.8 %psum.15 = f32[16,64]{1,0:T(8,128)S(1)} all-reduce(f32[16,64]{1,0:T(8,128)S(1)} %get-tuple-element.224), channel_id=1, replica_groups=mesh['seq'=8,'fsdp'=4] {'fsdp'}, use_global_device_ids=true, to_apply=%region_8.9 | all-reduce | flops 1024 | bytes 8192 | tf_op jit(solution)/shard_map/psum | solution.py:71
  170.2 10.7 %all-reduce.3.cloned.1.call-done = f32[16,64,128]{2,1,0:T(8,128)} async-done(((f32[16,64,128]{2,1,0:T(8,128)}), f32[16,64,128]{2,1,0:T(8,128)}) %all-reduce.3.cloned.1.call-update) | async-done | bytes 524304 | tf_op jit(solution)/shard_map/psum | solution.py:71
  183.1 5.5 all-to-all-start.1
  188.6 171.9 %all-gather.3.cloned.1.call-done = bf16[7168,2048]{1,0:T(8,128)(2,1)} async-done(((bf16[1792,2048]{1,0:T(8,128)(2,1)}), bf16[7168,2048]{1,0:T(8,128)(2,1)}) %all-gather.3.cloned.1.call-update) | async-done | bytes 29360144 | tf_op jit(solution)/shard_map/all_gather | solution.py:102
  360.5 12.8 %fusion.41 = f32[16,2048]{1,0:T(8,128)S(1)} fusion(bf16[16,7168]{1,0:T(8,128)(2,1)S(1)} %reshape.72, bf16[7168,2048]{1,0:T(8,128)(2,1)} %all-gather.3.cloned.1.call-done), kind=kOutput, calls=%fused_computation.68 | convolution fusion | flops 469762048 | bytes 29720576 | tf_op jit(solution)/shard_map/dot_general | solution.py:108
  373.3 166.8 %all-gather.5.cloned.1.call-done = bf16[7168,2048]{1,0:T(8,128)(2,1)} async-done(((bf16[1792,2048]{1,0:T(8,128)(2,1)}), bf16[7168,2048]{1,0:T(8,128)(2,1)}) %all-gather.5.cloned.1.call-update) | async-done | bytes 29360144 | tf_op jit(solution)/shard_map/all_gather | solution.py:103
  540.1 14.0 %fusion.18 = bf16[16,1792]{1,0:T(8,128)(2,1)S(1)} fusion(bf16[2048,1792]{1,0:T(8,128)(2,1)} %param.21, bf16[16,7168]{1,0:T(8,128)(2,1)S(1)} %reshape.72, bf16[7168,2048]{1,0:T(8,128)(2,1)} %all-gather.5.cloned.1.call-done, f32[16,2048]{1,0:T(8,128)S(1)} %fusion.41), kind=kOutput, calls=%fused_computation.31 | convolution fusion | flops 587427840 | bytes 37117952 | tf_op jit(solution)/shard_map/dot_general | solution.py:111
  554.8 5.5 all-to-all-start.3
  560.5 6.7 %all-to-all-done.3 = bf16[8,2,1792]{2,1,0:T(2,128)(2,1)S(1)} async-done(((bf16[8,2,1792]{2,1,0:T(2,128)(2,1)}), bf16[8,2,1792]{2,1,0:T(2,128)(2,1)S(1)}, u32[]{:S(2)}, u32[]{:S(2)}) %all-to-all-start.3) | async-done | bytes 57376 | tf_op jit(solution)/shard_map/all_to_all | solution.py:115
  (218 shorter events, 88.5 us)
Async XLA Ops:
  7.2 33.0 %all-to-all-start = ((bf16[8,8,8192]{2,0,1:T(8,128)(2,1)}), bf16[8,8,8192]{2,0,1:T(8,128)(2,1)S(1)}, u32[]{:S(2)}, u32[]{:S(2)}) async-start(bf16[8,8,8192]{2,0,1:T(8,128)(2,1)} %bitcast.74), calls=%async_computation | async-start | bytes 2097152 | tf_op jit(solution)/shard_map/all_to_all | solution.py:21
  14.4 166.4 %all-reduce.3.cloned.1.call-start = ((), (), s32[]{:S(2)}) async-start(), calls=%async_computation.4 | async-start | bytes 1048576 | tf_op jit(solution)/shard_map/psum | solution.py:71
  148.3 1.5 copy-start.2
  148.3 1.9 copy-start
  148.3 2.1 copy-start.1
  148.3 8.0 %copy-start.3 = (f32[8,8]{1,0:T(8,128)S(1)}, f32[8,8]{1,0:T(8,128)}, u32[]{:S(2)}) copy-start(f32[8,8]{1,0:T(8,128)} %param.18) | copy-start | bytes 772
  148.3 212.2 %all-gather.3.cloned.1.call-start = ((), (), s32[]{:S(2)}) async-start(), calls=%async_computation.5 | async-start | bytes 36700160 | tf_op jit(solution)/shard_map/all_gather | solution.py:102
  149.1 391.0 %all-gather.5.cloned.1.call-start = ((), (), s32[]{:S(2)}) async-start(), calls=%async_computation.6 | async-start | bytes 36700160 | tf_op jit(solution)/shard_map/all_gather | solution.py:103
  151.5 12.8 %all-to-all-start.2 = ((bf16[8,2,7168]{2,1,0:T(2,128)(2,1)}), bf16[8,2,7168]{2,1,0:T(2,128)(2,1)S(1)}, u32[]{:S(2)}, u32[]{:S(2)}) async-start(bf16[8,2,7168]{2,1,0:T(2,128)(2,1)} %reshape_reshape.3), calls=%async_computation.2 | async-start | bytes 458752 | tf_op jit(solution)/shard_map/all_to_all | solution.py:105
  183.1 371.7 %all-to-all-start.1 = ((bf16[8,8,2048]{2,1,0:T(8,128)(2,1)}), bf16[8,8,2048]{2,1,0:T(8,128)(2,1)S(1)}, u32[]{:S(2)}, u32[]{:S(2)}) async-start(bf16[8,8,2048]{2,1,0:T(8,128)(2,1)} %all_to_all.35), calls=%async_computation.1 | async-start | bytes 524288 | tf_op jit(solution)/shard_map/all_to_all | solution.py:74
  554.8 12.4 %all-to-all-start.3 = ((bf16[8,2,1792]{2,1,0:T(2,128)(2,1)}), bf16[8,2,1792]{2,1,0:T(2,128)(2,1)S(1)}, u32[]{:S(2)}, u32[]{:S(2)}) async-start(bf16[8,2,1792]{2,1,0:T(2,128)(2,1)} %reshape.73), calls=%async_computation.3 | async-start | bytes 114688 | tf_op jit(solution)/shard_map/all_to_all | solution.py:115
Sparse Core Ops, SparseCore 0:
  148.4 32.3 all-reduce.2
  182.4 177.9 all-gather.2
  362.1 177.9 all-gather.4
where the time goes:
time: 578 us; the launch traced here: 575 us
  waiting for transfers between devices  391 us (68%)
  matrix products  84.9 us (15%)
  other arithmetic  27.3 us (5%)
  starting transfers between devices  23.2 us (4%)
  local copies, waits for them, and re-layouts  23.1 us (4%)
  between operations  13.9 us (2%)
  blocking collectives  11.5 us (2%)
    all_gather x1, waiting for transfers between devices, on_device(): lax.all_gather(gate_weight, 'fsdp', axis=0, tiled=True)  172 us
    all_gather x1, waiting for transfers between devices, on_device(): lax.all_gather(up_weight, 'fsdp', axis=0, tiled=True)  167 us
    dot_general x16, matrix products, head_values(): lax.dot_general(weights_row[:, quarter:], stored[QK_DIM:], contract, pref...  31.2 us
    all_to_all x1, waiting for transfers between devices, on_device(): lax.all_to_all(projected, 'seq', split_axis=1, concat_axis=0, tiled=True)  25.6 us
    dot_general x16, matrix products, one_block(): jnp.dot(queries, stored[:QK_DIM], preferred_element_type=jnp.float32)  21.7 us
    dynamic_update_slice x16, other arithmetic, on_device(): scores = lax.map(head_scores, (heads_major, cached))  15.8 us
    squeeze x16, local copies, waits for them, and re-layouts, on_device(): weighted = lax.map(head_values, (weights_bf, heads_major, cached))  15.4 us
    dot_general x1, matrix products, on_device(): jnp.dot(hidden, down_weight, preferred_element_type=jnp.float32)  14 us
  transfers between devices with their start and end apart: 7, of which 6 were waited for; matrix products, arithmetic and copies ran while one was open for 5% of the time, Pallas kernels for 0%

commit v1 on v0

--- a/solution.py
+++ b/solution.py
@@ -14,7 +14,6 @@
 def on_device(
     projected, cached, stream, norm_gain, routes, route_gates, gate_weight, up_weight, down_weight
 ):
-    shard_set = (gate_weight, up_weight)
     pack_width = 2 * QK_DIM + V_DIM
     heads_here = cached.shape[0]
     cache_len = cached.shape[2]
@@ -74,7 +73,6 @@
     attention = lax.all_to_all(merged, "seq", split_axis=0, concat_axis=1, tiled=True)
     tokens = stream.astype(jnp.float32)
     tok_count = tokens.shape[0]
-    width_full = tokens.shape[1]
     slice_cols = gate_weight.shape[0]
     normed = (
         tokens * lax.rsqrt(jnp.mean(tokens * tokens, axis=1, keepdims=True) + 1e-06) * norm_gain
@@ -93,20 +91,19 @@
         placed_flat.astype(jnp.bfloat16), normed, preferred_element_type=jnp.float32
     ).astype(jnp.bfloat16)
     group_size = lax.axis_size("seq") // WAVE_EXPERTS
+    send_rows = lax.dynamic_slice_in_dim(
+        send_rows, lax.axis_index("fsdp") * slice_cols, slice_cols, 1
+    )
     outgoing = jnp.broadcast_to(
-        send_rows.reshape(WAVE_EXPERTS, 1, CAPACITY, width_full),
-        (WAVE_EXPERTS, group_size, CAPACITY, width_full),
+        send_rows.reshape(WAVE_EXPERTS, 1, CAPACITY, slice_cols),
+        (WAVE_EXPERTS, group_size, CAPACITY, slice_cols),
     )
-    outgoing = outgoing.reshape(WAVE_EXPERTS * group_size, CAPACITY, width_full)
-    shard_set = (
-        lax.all_gather(gate_weight, "fsdp", axis=0, tiled=True),
-        lax.all_gather(up_weight, "fsdp", axis=0, tiled=True),
-    )
+    outgoing = outgoing.reshape(WAVE_EXPERTS * group_size, CAPACITY, slice_cols)
     received = lax.all_to_all(outgoing, "seq", split_axis=0, concat_axis=0, tiled=True)
     rows_in = received.reshape(-1, received.shape[2])
-    full_gate, full_up = shard_set
-    gate_act = jnp.dot(rows_in, full_gate, preferred_element_type=jnp.float32)
-    upward = jnp.dot(rows_in, full_up, preferred_element_type=jnp.float32)
+    gate_act = jnp.dot(rows_in, gate_weight, preferred_element_type=jnp.float32)
+    upward = jnp.dot(rows_in, up_weight, preferred_element_type=jnp.float32)
+    gate_act, upward = lax.psum((gate_act, upward), "fsdp")
     hidden = (jax.nn.silu(gate_act) * upward).astype(jnp.bfloat16)
     partial_value = jnp.dot(hidden, down_weight, preferred_element_type=jnp.float32).astype(
         jnp.bfloat16

time: 578 us -> 236 us (0.41)
  waiting for transfers between devices: 391 us -> 58 us
  matrix products: 84.9 us -> 69.9 us
  blocking collectives: 11.5 us -> 26.4 us
  starting transfers between devices: 23.2 us -> 13.5 us
    all_gather x2 -> x0, waiting for transfers between devices: 339 us -> none  [the longest x1 172 us: on_device(): lax.all_gather(gate_weight, 'fsdp', axis=0, tiled=True)]
    psum x1, waiting for transfers between devices: 10.7 us -> 27.5 us  [on_device(): weighted, key_total = lax.psum((weighted, key_total), 'fsdp')]
    all_to_all x0 -> x1, blocking collectives: none -> 13.9 us  [on_device(): lax.all_to_all(outgoing, 'seq', split_axis=0, concat_axis=0, tiled=True)]
    dot_general x1, matrix products: 14 us -> 4.35 us  [on_device(): jnp.dot(hidden, down_weight, preferred_element_type=jnp.float32)]
    all_to_all x1 -> x0, waiting for transfers between devices: 7.83 us -> none  [on_device(): lax.all_to_all(outgoing, 'seq', split_axis=0, concat_axis=0, tiled=True)]
    all_to_all x1, waiting for transfers between devices: 25.6 us -> 17.9 us  [on_device(): lax.all_to_all(projected, 'seq', split_axis=1, concat_axis=0, tiled=True)]
    all_to_all x1, waiting for transfers between devices: 0.01 us -> 6.95 us  [on_device(): lax.all_to_all(merged, 'seq', split_axis=0, concat_axis=1, tiled=True)]
    dot_general x1 -> x2, matrix products: 12.8 us -> 6.66 us  [the longest x1 4.94 us: on_device(): gate_act = jnp.dot(rows_in, gate_weight, preferred_element_type=jnp.float32)]
  transfers between devices with their start and end apart: 7 -> 4, of which waited for: 6 -> 4; matrix products, arithmetic and copies ran while one was open for 5% -> 4% of each run, Pallas kernels for 0% -> 0%
where the time goes in v1:
time: 236 us; the launch traced here: 234 us
  matrix products  69.9 us (30%)
  waiting for transfers between devices  58 us (25%)
  other arithmetic  27.9 us (12%)
  blocking collectives  26.4 us (11%)
  local copies, waits for them, and re-layouts  23.6 us (10%)
  between operations  14.2 us (6%)
  starting transfers between devices  13.5 us (6%)
    dot_general x16, matrix products, head_values(): lax.dot_general(weights_row[:, quarter:], stored[QK_DIM:], contract, pref...  31.2 us
    psum x1, waiting for transfers between devices, on_device(): weighted, key_total = lax.psum((weighted, key_total), 'fsdp')  27.5 us
    dot_general x16, matrix products, one_block(): jnp.dot(queries, stored[:QK_DIM], preferred_element_type=jnp.float32)  21.7 us
    all_to_all x1, waiting for transfers between devices, on_device(): lax.all_to_all(projected, 'seq', split_axis=1, concat_axis=0, tiled=True)  17.9 us
    dynamic_update_slice x16, other arithmetic, on_device(): scores = lax.map(head_scores, (heads_major, cached))  15.8 us
    squeeze x16, local copies, waits for them, and re-layouts, on_device(): weighted = lax.map(head_values, (weights_bf, heads_major, cached))  15.4 us
    all_to_all x1, blocking collectives, on_device(): lax.all_to_all(outgoing, 'seq', split_axis=0, concat_axis=0, tiled=True)  13.9 us
    all_to_all x1, waiting for transfers between devices, on_device(): lax.all_to_all(merged, 'seq', split_axis=0, concat_axis=1, tiled=True)  6.95 us
  transfers between devices with their start and end apart: 4, of which 4 were waited for; matrix products, arithmetic and copies ran while one was open for 4% of the time, Pallas kernels for 0%

profile of v1, /device:TPU:0, one launch (start us, length us, event | category | flops | bytes accessed | tf_op | source)
XLA Modules:
  0.0 233.8 jit_solution(6754494239887515419)
XLA Ops:
  10.6 13.9 %all_to_all.45 = bf16[8,2,1792]{2,1,0:T(2,128)(2,1)S(1)} all-to-all(bf16[8,2,1792]{2,1,0:T(2,128)(2,1)S(1)} %reshape_reshape.3), channel_id=1, replica_groups=mesh['seq'=8,'fsdp'=4] {'seq'}, dimensions={0} | all-to-all | bytes 114688 | tf_op jit(solution)/shard_map/all_to_all | solution.py:102
  24.5 4.5 %all-to-all-start = ((bf16[8,8,8192]{2,0,1:T(8,128)(2,1)}), bf16[8,8,8192]{2,0,1:T(8,128)(2,1)}, u32[]{:S(2)}, u32[]{:S(2)}) async-start(bf16[8,8,8192]{2,0,1:T(8,128)(2,1)} %bitcast.75), calls=%async_computation | async-start | bytes 2097152 | tf_op jit(solution)/shard_map/all_to_all | solution.py:20
  29.2 4.9 %fusion.34 = f32[16,2048]{1,0:T(8,128)} fusion(bf16[16,1792]{1,0:T(8,128)(2,1)S(1)} %reshape.72, bf16[1792,2048]{1,0:T(8,128)(2,1)} %param.19), kind=kOutput, calls=%fused_computation.62 | convolution fusion | flops 117440512 | bytes 7528448 | tf_op jit(solution)/shard_map/dot_general | solution.py:104
  35.9 17.9 %all-to-all-done = bf16[8,8,8192]{2,0,1:T(8,128)(2,1)} async-done(((bf16[8,8,8192]{2,0,1:T(8,128)(2,1)}), bf16[8,8,8192]{2,0,1:T(8,128)(2,1)}, u32[]{:S(2)}, u32[]{:S(2)}) %all-to-all-start) | async-done | bytes 1048608 | tf_op jit(solution)/shard_map/all_to_all | solution.py:20
  56.0 42.4 %while.30 = (s32[]{:T(128)}, f32[16,64,1808]{2,1,0:T(8,128)}, bf16[16,64,512]{2,1,0:T(8,128)(2,1)S(1)}, s32[]{:T(128)}, bf16[16,320,1792]{2,1,0:T(8,128)(2,1)}) while((s32[]{:T(128)}, f32[16,64,1808]{2,1,0:T(8,128)}, bf16[16,64,512]{2,1,0:T(8,128)(2,1)S(1)}, s32[]{:T(128)}, bf16[16,320,1792]{2,1,0:T(8,128)(2,1)}) %tuple.67), condition=%wide.region_1.2_spmd.clone, body=%wide.region_0.1_spmd.sunk.clone | while | flops 44664832 | bytes 2368581 | solution.py:47
  98.4 4.1 %select_reduce_fusion = f32[16,64]{1,0:T(8,128)S(1)} fusion(f32[16,64,1808]{2,1,0:T(8,128)} %get-tuple-element.154, pred[64,1808]{1,0:T(8,128)(4,1)S(1)} %concatenate.9), kind=kLoop, calls=%fused_computation.24 | loop fusion | flops 3701760 | bytes 7525376 | tf_op jit(solution)/shard_map/reduce_max | solution.py:53
  102.5 5.8 %pmax.7 = f32[16,64]{1,0:T(8,128)S(1)} all-reduce(f32[16,64]{1,0:T(8,128)S(1)} %select_reduce_fusion), channel_id=1, replica_groups=mesh['seq'=8,'fsdp'=4] {'fsdp'}, use_global_device_ids=true, to_apply=%region_3.4 | all-reduce | flops 1024 | bytes 8192 | tf_op jit(solution)/shard_map/pmax | solution.py:53
  108.2 5.7 %fusion.14 = (f32[16,64]{1,0:T(8,128)S(1)}, bf16[16,64,1808]{2,1,0:T(8,128)(2,1)}) fusion(f32[16,64,1808]{2,1,0:T(8,128)} %get-tuple-element.154, f32[16,64]{1,0:T(8,128)S(1)} %pmax.7, pred[64,1808]{1,0:T(8,128)(4,1)S(1)} %concatenate.9), kind=kLoop, calls=%fused_computation.25 | loop fusion | flops 9255936 | bytes 11232256 | tf_op jit(solution)/shard_map/reduce_sum | solution.py:55
  113.9 49.2 %while.31 = (s32[]{:T(128)}, f32[16,64,128]{2,1,0:T(8,128)}, bf16[16,64,1808]{2,1,0:T(8,128)(2,1)}, bf16[16,64,512]{2,1,0:T(8,128)(2,1)S(1)}, s32[]{:T(128)}, /*index=5*/bf16[16,320,1792]{2,1,0:T(8,128)(2,1)}) while((s32[]{:T(128)}, f32[16,64,128]{2,1,0:T(8,128)}, bf16[16,64,1808]{2,1,0:T(8,128)(2,1)}, ...), condition=%wide.region_5.6_spmd.clone, body=%wide.region_4.5_spmd.sunk.clone | while | flops 29630468 | bytes 1434721 | solution.py:69
  115.1 1.9 fusion.67
  130.4 1.9 fusion.67
  133.5 1.9 fusion.67
  139.6 1.9 fusion.67
  142.7 2.0 fusion.67
  148.9 2.0 fusion.67
  155.0 2.0 fusion.67
  161.2 2.0 fusion.67
  163.1 6.7 %psum.29 = f32[16,64]{1,0:T(8,128)S(1)} all-reduce(f32[16,64]{1,0:T(8,128)S(1)} %get-tuple-element.227), channel_id=1, replica_groups=mesh['seq'=8,'fsdp'=4] {'fsdp'}, use_global_device_ids=true, to_apply=%region_8.9 | all-reduce | flops 1024 | bytes 8192 | tf_op jit(solution)/shard_map/psum | solution.py:70
  169.9 27.5 %all-reduce.4.cloned.1.call-done = (f32[16,64,128]{2,1,0:T(8,128)}, f32[16,2048]{1,0:T(8,128)}, f32[16,2048]{1,0:T(8,128)}) async-done(((f32[16,64,128]{2,1,0:T(8,128)}, f32[16,2048]{1,0:T(8,128)}, f32[16,2048]{1,0:T(8,128)}), (f32[16,64,128]{2,1,0:T(8,128)}, f32[16,2048]{1,0:T(8,128)}, f32[16,2048]{1,0:T(8,128)})) %all-reduce.4.cloned.1.call-update) | async-done | bytes 786448 | tf_op jit(solution)/shard_map/psum | solution.py:70
  197.3 4.3 %convolution_convert_fusion = bf16[16,1792]{1,0:T(8,128)(2,1)S(1)} fusion(bf16[2048,1792]{1,0:T(8,128)(2,1)} %param.21, f32[16,2048]{1,0:T(8,128)} %get-tuple-element.223, f32[16,2048]{1,0:T(8,128)} %get-tuple-element.224), kind=kOutput, calls=%fused_computation.27 | convolution fusion | flops 117665792 | bytes 7659520 | tf_op jit(solution)/shard_map/dot_general | solution.py:108
  202.3 5.5 %all-to-all-start.3 = ((bf16[8,2,1792]{2,1,0:T(2,128)(2,1)}), bf16[8,2,1792]{2,1,0:T(2,128)(2,1)S(1)}, u32[]{:S(2)}, u32[]{:S(2)}) async-start(bf16[8,2,1792]{2,1,0:T(2,128)(2,1)} %reshape.73), calls=%async_computation.3 | async-start | bytes 114688 | tf_op jit(solution)/shard_map/all_to_all | solution.py:112
  209.1 5.6 %all-to-all-done.3 = bf16[8,2,1792]{2,1,0:T(2,128)(2,1)S(1)} async-done(((bf16[8,2,1792]{2,1,0:T(2,128)(2,1)}), bf16[8,2,1792]{2,1,0:T(2,128)(2,1)S(1)}, u32[]{:S(2)}, u32[]{:S(2)}) %all-to-all-start.3) | async-done | bytes 57376 | tf_op jit(solution)/shard_map/all_to_all | solution.py:112
  214.7 3.4 %all-to-all-start.1 = ((bf16[8,8,2048]{2,1,0:T(8,128)(2,1)}), bf16[8,8,2048]{2,1,0:T(8,128)(2,1)S(1)}, u32[]{:S(2)}, u32[]{:S(2)}) async-start(bf16[8,8,2048]{2,1,0:T(8,128)(2,1)} %all_to_all.35), calls=%async_computation.1 | async-start | bytes 524288 | tf_op jit(solution)/shard_map/all_to_all | solution.py:73
  219.3 6.9 %all-to-all-done.1 = bf16[8,8,2048]{2,1,0:T(8,128)(2,1)S(1)} async-done(((bf16[8,8,2048]{2,1,0:T(8,128)(2,1)}), bf16[8,8,2048]{2,1,0:T(8,128)(2,1)S(1)}, u32[]{:S(2)}, u32[]{:S(2)}) %all-to-all-start.1) | async-done | bytes 262176 | tf_op jit(solution)/shard_map/all_to_all | solution.py:73
  (216 shorter events, 86.8 us)
Async XLA Ops:
  24.5 9.6 %slice-start = ((s8[7340032]{0:T(1024)(128)(4,1)}), s8[3145728]{0:T(1024)(128)(4,1)S(1)}, s32[]{:S(2)}) async-start(s8[7340032]{0:T(1024)(128)(4,1)} %bitcast.72), calls=%async_computation.5 | async-start | bytes 6291456
  24.5 29.3 %all-to-all-start = ((bf16[8,8,8192]{2,0,1:T(8,128)(2,1)}), bf16[8,8,8192]{2,0,1:T(8,128)(2,1)}, u32[]{:S(2)}, u32[]{:S(2)}) async-start(bf16[8,8,8192]{2,0,1:T(8,128)(2,1)} %bitcast.75), calls=%async_computation | async-start | bytes 2097152 | tf_op jit(solution)/shard_map/all_to_all | solution.py:20
  29.0 168.3 %all-reduce.4.cloned.1.call-start = ((), (), s32[]{:S(2)}) async-start(), calls=%async_computation.4 | async-start | bytes 1572864 | tf_op jit(solution)/shard_map/psum | solution.py:70
  29.2 5.0 %slice-start.1 = ((s8[7340032]{0:T(1024)(128)(4,1)}), s8[4194304]{0:T(1024)(128)(4,1)S(1)}, s32[]{:S(2)}) async-start(s8[7340032]{0:T(1024)(128)(4,1)} %bitcast.72), calls=%async_computation.6 | async-start | bytes 8388608
  113.9 104.2 %copy-start.1 = (s32[8,8]{1,0:T(8,128)S(1)}, s32[8,8]{1,0:T(8,128)}, u32[]{:S(2)}) copy-start(s32[8,8]{1,0:T(8,128)} %param.17) | copy-start | bytes 772
  113.9 104.2 %copy-start.2 = (f32[8,8]{1,0:T(8,128)S(1)}, f32[8,8]{1,0:T(8,128)}, u32[]{:S(2)}) copy-start(f32[8,8]{1,0:T(8,128)} %param.18) | copy-start | bytes 772
  197.3 10.5 %copy-start = (f32[16,64,128]{2,1,0:T(8,128)S(1)}, f32[16,64,128]{2,1,0:T(8,128)}, u32[]{:S(2)}) copy-start(f32[16,64,128]{2,1,0:T(8,128)} %get-tuple-element.222) | copy-start | bytes 1572868
  202.3 12.4 %all-to-all-start.3 = ((bf16[8,2,1792]{2,1,0:T(2,128)(2,1)}), bf16[8,2,1792]{2,1,0:T(2,128)(2,1)S(1)}, u32[]{:S(2)}, u32[]{:S(2)}) async-start(bf16[8,2,1792]{2,1,0:T(2,128)(2,1)} %reshape.73), calls=%async_computation.3 | async-start | bytes 114688 | tf_op jit(solution)/shard_map/all_to_all | solution.py:112
  214.7 11.6 %all-to-all-start.1 = ((bf16[8,8,2048]{2,1,0:T(8,128)(2,1)}), bf16[8,8,2048]{2,1,0:T(8,128)(2,1)S(1)}, u32[]{:S(2)}, u32[]{:S(2)}) async-start(bf16[8,8,2048]{2,1,0:T(8,128)(2,1)} %all_to_all.35), calls=%async_computation.1 | async-start | bytes 524288 | tf_op jit(solution)/shard_map/all_to_all | solution.py:73
Sparse Core Ops, SparseCore 0:
  163.3 34.0 all-reduce.3

commit v2 on v1

--- a/solution.py
+++ b/solution.py
@@ -1,8 +1,11 @@
+import functools
 import math
 
 import jax
 import jax.numpy as jnp
 from jax import lax
+from jax.experimental import pallas as pl
+from jax.experimental.pallas import tpu as pltpu
 from jax.sharding import PartitionSpec as P
 
 QK_DIM = 192
@@ -124,6 +127,357 @@
     return (attention, routed)
 
 
+MESH = pl.DeviceIdType.MESH
+GROUP = 4
+LOG2E = 1.4426950408889634
+
+
+def one_kernel(
+    n_seq,
+    proj, cached, stream, gain, routes, gates, gate_w, up_w, down_w,
+    att_out, routed_out,
+    gath, q_buf, k_span, v_span, cache_v, gate_v, up_v, down_v,
+    rows_out, rows_in, part, part_in, hid, down_out, down_in,
+    o_own, o_buf, o_in, st_buf, st_in, fin, hop,
+    load_sem, own_sem,
+    rows_s, rows_r, proj_s, proj_r, q_s, q_r, part_s, part_r, hid_s, hid_r,
+    dn_s, dn_r, o_s, o_r, st_s, st_r, fin_s, fin_r, hop_s, hop_r,
+):
+    f32, bf16 = jnp.float32, jnp.bfloat16
+    s = lax.axis_index("seq")
+    f = lax.axis_index("fsdp")
+    f1 = f + 1 - 2 * lax.rem(f, 2)
+    f2 = lax.rem(f + 2, 4)
+    f3 = lax.rem(f1 + 2, 4)
+    peers = (f, f1, f2, f3)
+    width = stream.shape[1]
+    cols = down_w.shape[1]
+    heads = cached.shape[0] // GROUP
+    pack = 2 * QK_DIM + V_DIM
+    chunk_cols = heads * pack
+    quarter = gate_w.shape[1] // GROUP
+    toks = stream.shape[0]
+    span = n_seq * toks
+    scale2 = LOG2E / math.sqrt(QK_DIM)
+
+    def remote(src, dst, ssem, rsem, seq_id, fs_id):
+        return pltpu.make_async_remote_copy(
+            src_ref=src, dst_ref=dst, send_sem=ssem, recv_sem=rsem,
+            device_id=(seq_id, fs_id), device_id_type=MESH,
+        )
+
+    own_proj = pltpu.make_async_copy(
+        proj.at[:, pl.ds(pl.multiple_of((s * GROUP + f) * chunk_cols, 128), chunk_cols)],
+        gath.at[s], own_sem,
+    )
+    own_proj.start()
+    loads = [
+        pltpu.make_async_copy(gate_w, gate_v, load_sem.at[0]),
+        pltpu.make_async_copy(up_w, up_v, load_sem.at[1]),
+        pltpu.make_async_copy(down_w, down_v, load_sem.at[2]),
+    ]
+    cache_loads = []
+    for x in range(GROUP):
+        piece = pl.ds(peers[x] * heads, heads)
+        cache_loads.append(
+            pltpu.make_async_copy(cached.at[piece], cache_v.at[piece], load_sem.at[3 + x])
+        )
+    for copy in (loads[0], loads[1], cache_loads[0], cache_loads[1], loads[2],
+                 cache_loads[2], cache_loads[3]):
+        copy.start()
+
+    barrier = pltpu.get_barrier_semaphore()
+    for k in range(1, n_seq):
+        pl.semaphore_signal(
+            barrier, inc=1, device_id=(lax.rem(s + k, n_seq), f), device_id_type=MESH
+        )
+    for x in range(1, GROUP):
+        pl.semaphore_signal(barrier, inc=1, device_id=(s, peers[x]), device_id_type=MESH)
+
+    tokens = stream[...].astype(f32)
+    inv = lax.rsqrt(jnp.sum(tokens * tokens, axis=1, keepdims=True) / width + 1e-06)
+    here = pl.ds(pl.multiple_of(f * cols, 128), cols)
+    normed = (stream[:, here].astype(f32) * inv * gain[:, here]).astype(bf16).astype(f32)
+    slots = WAVE_EXPERTS * CAPACITY
+    lane = lax.broadcasted_iota(jnp.int32, (toks, 128), 1)
+    row = lax.broadcasted_iota(jnp.int32, (toks, 128), 0)
+    lane_expert = lane // CAPACITY
+    hits = jnp.zeros((toks, 128), f32)
+    weight_of = jnp.zeros((toks, 128), f32)
+    route_vals = routes[...]
+    gate_vals = gates[...]
+    for j in range(routes.shape[1]):
+        match = route_vals[:, j : j + 1] == lane_expert
+        hits = hits + jnp.where(match, 1.0, 0.0)
+        weight_of = weight_of + jnp.where(match, gate_vals[:, j : j + 1], 0.0)
+    rank = jnp.zeros((toks, 128), f32) - 1.0
+    for t in range(toks):
+        rank = rank + jnp.where(row >= t, hits[t : t + 1, :], 0.0)
+    slot_of = (lane % CAPACITY).astype(f32)
+    placed = jnp.where((hits == 1.0) & (rank == slot_of), 1.0, 0.0)
+    mix = placed * weight_of
+    for r in range(slots):
+        rows_out[r // CAPACITY, r % CAPACITY : r % CAPACITY + 1, :] = jnp.sum(
+            placed[:, r : r + 1] * normed, axis=0, keepdims=True
+        )
+    rows_in[s] = rows_out[s]
+
+    pl.semaphore_wait(barrier, n_seq - 1 + GROUP - 1)
+
+    rows_c, proj_c = [], []
+    for k in range(1, n_seq):
+        to = lax.rem(s + k, n_seq)
+        rows_c.append(remote(rows_out.at[to], rows_in.at[s], rows_s.at[k], rows_r.at[k], to, f))
+        rows_c[-1].start()
+    for k in range(1, n_seq):
+        to = lax.rem(s + k, n_seq)
+        start = pl.multiple_of((to * GROUP + f) * chunk_cols, 128)
+        proj_c.append(
+            remote(proj.at[:, pl.ds(start, chunk_cols)], gath.at[s],
+                   proj_s.at[k], proj_r.at[k], to, f)
+        )
+        proj_c[-1].start()
+
+    for c in rows_c:
+        c.wait_recv()
+    rows = jnp.concatenate([rows_in[i] for i in range(n_seq)], axis=0).astype(bf16)
+    loads[0].wait()
+    loads[1].wait()
+    part_c = []
+    for x in (3, 2, 1, 0):
+        block = pl.ds(pl.multiple_of(peers[x] * quarter, 128), quarter)
+        part[x, :, :quarter] = jnp.dot(rows, gate_v[:, block], preferred_element_type=f32)
+        part[x, :, quarter:] = jnp.dot(rows, up_v[:, block], preferred_element_type=f32)
+        if x:
+            c = remote(part.at[x], part_in.at[x], part_s.at[x], part_r.at[x], s, peers[x])
+            c.start()
+            part_c.append(c)
+
+    own_proj.wait()
+    for c in proj_c:
+        c.wait_recv()
+    for h in range(heads):
+        base = h * pack
+        q = gath[:, :, base : base + QK_DIM].astype(f32).reshape(span, QK_DIM)
+        q_buf[f, h] = q.astype(bf16)
+        wide = gath[:, :, base + 128 : base + 384].astype(f32).reshape(span, 256)
+        k_span[h] = pltpu.roll(wide, 256 - (QK_DIM - 128), 1)[:, :QK_DIM].astype(bf16)
+        v = gath[:, :, base + 2 * QK_DIM : base + pack].astype(f32).reshape(span, V_DIM)
+        v_span[h] = v.astype(bf16)
+    q_c = []
+    for x in (2, 1):
+        q_c.append(remote(q_buf.at[f], q_buf.at[f], q_s.at[x], q_r.at[x], s, peers[x]))
+        q_c[-1].start()
+
+    nt = (((1,), (1,)), ((), ()))
+    st_lane = lax.broadcasted_iota(jnp.int32, (span, 128), 1)
+
+    def attend(x):
+        cache_loads[x].wait()
+
+        def one_head(h, stats):
+            head = peers[x] * heads + h
+            q = q_buf[peers[x], h]
+            scores = jnp.dot(q, cache_v[head, :QK_DIM, :], preferred_element_type=f32)
+            top = jnp.max(scores, axis=1, keepdims=True)
+            if x == 0:
+                near = lax.dot_general(q, k_span[h], nt, preferred_element_type=f32)
+                open_at = lax.broadcasted_iota(
+                    jnp.int32, (span, span), 1
+                ) <= lax.broadcasted_iota(jnp.int32, (span, span), 0)
+                near = jnp.where(open_at, near, -jnp.inf)
+                top = jnp.maximum(top, jnp.max(near, axis=1, keepdims=True))
+            expw = jnp.exp2((scores - top) * scale2)
+            total = jnp.sum(expw, axis=1, keepdims=True)
+            out = lax.dot_general(
+                expw.astype(bf16), cache_v[head, QK_DIM:, :], nt, preferred_element_type=f32
+            )
+            if x == 0:
+                near_w = jnp.exp2((near - top) * scale2)
+                total = total + jnp.sum(near_w, axis=1, keepdims=True)
+                out = out + jnp.dot(near_w.astype(bf16), v_span[h], preferred_element_type=f32)
+            out = out / total
+            if x == 0:
+                o_own[h] = out
+            else:
+                o_buf[x, h] = out.astype(bf16)
+            stats = jnp.where(st_lane == h, top, stats)
+            return jnp.where(st_lane == heads + h, total, stats)
+
+        st_buf[x] = lax.fori_loop(0, heads, one_head, jnp.zeros((span, 128), f32))
+        if x:
+            pair = [
+                remote(o_buf.at[x], o_in.at[x], o_s.at[x], o_r.at[x], s, peers[x]),
+                remote(st_buf.at[x], st_in.at[x], st_s.at[x], st_r.at[x], s, peers[x]),
+            ]
+            for c in pair:
+                c.start()
+            return pair
+        return []
+
+    attend(0)
+
+    for c in part_c:
+        c.wait_recv()
+    both = part[0] + part_in[1] + part_in[2] + part_in[3]
+    gate_act = both[:, :quarter]
+    hid[f] = (gate_act / (1.0 + jnp.exp(-gate_act)) * both[:, quarter:]).astype(bf16)
+    hid_c = []
+    for x in (3, 2, 1):
+        hid_c.append(remote(hid.at[f], hid.at[f], hid_s.at[x], hid_r.at[x], s, peers[x]))
+        hid_c[-1].start()
+
+    q_c[0].wait_recv()
+    q_c.append(remote(q_buf.at[f2], q_buf.at[f2], q_s.at[3], q_r.at[3], s, f1))
+    q_c[-1].start()
+    q_c[1].wait_recv()
+    o_c = attend(1)
+
+    for c in hid_c:
+        c.wait_recv()
+    loads[2].wait()
+    acc = jnp.zeros((n_seq * CAPACITY, cols), f32)
+    for j in range(GROUP):
+        acc = acc + jnp.dot(
+            hid[j], down_v[j * quarter : (j + 1) * quarter, :], preferred_element_type=f32
+        )
+    acc = acc.astype(bf16).astype(f32)
+    for i in range(n_seq):
+        down_out[i] = acc[i * CAPACITY : (i + 1) * CAPACITY, :]
+    down_in[s] = down_out[s]
+    dn_c = []
+    for k in range(1, n_seq):
+        to = lax.rem(s + k, n_seq)
+        dn_c.append(remote(down_out.at[to], down_in.at[s], dn_s.at[k], dn_r.at[k], to, f))
+        dn_c[-1].start()
+
+    o_c += attend(2)
+    q_c[2].wait_recv()
+    o_c += attend(3)
+
+    for c in dn_c:
+        c.wait_recv()
+    mixed = jnp.zeros((toks, cols), f32)
+    for r in range(slots):
+        mixed = mixed + mix[:, r : r + 1] * down_in[
+            r // CAPACITY, r % CAPACITY : r % CAPACITY + 1, :
+        ]
+    routed_out[...] = mixed.astype(bf16)
+
+    for c in o_c:
+        c.wait_recv()
+    stat = [st_buf[0]] + [st_in[x] for x in (1, 2, 3)]
+    for h in range(heads):
+        tops = [v[:, h : h + 1] for v in stat]
+        totals = [v[:, heads + h : heads + h + 1] for v in stat]
+        top = jnp.maximum(jnp.maximum(tops[0], tops[1]), jnp.maximum(tops[2], tops[3]))
+        share = [t * jnp.exp2((m - top) * scale2) for t, m in zip(totals, tops)]
+        whole = share[0] + share[1] + share[2] + share[3]
+        out = o_own[h] * share[0]
+        for x in (1, 2, 3):
+            out = out + o_in[x, h].astype(f32) * share[x]
+        out = (out / whole).reshape(n_seq, toks, V_DIM).astype(bf16)
+        fin[:, :, h * V_DIM : (h + 1) * V_DIM] = out
+    hop[f, s] = fin[s]
+    fin_c, hop_c = [], []
+    for k in range(1, n_seq):
+        to = lax.rem(s + k, n_seq)
+        fin_c.append(remote(fin.at[to], hop.at[f, s], fin_s.at[k], fin_r.at[k], to, f))
+        fin_c[-1].start()
+    for c in fin_c:
+        c.wait_recv()
+    for x in (3, 2, 1):
+        hop_c.append(remote(hop.at[f], hop.at[f], hop_s.at[x], hop_r.at[x], s, peers[x]))
+        hop_c[-1].start()
+    for c in hop_c:
+        c.wait_recv()
+    block = heads * V_DIM
+    for r in range(n_seq):
+        for j in range(GROUP):
+            at = (r * GROUP + j) * block
+            att_out[:, at : at + block] = hop[j, r]
+    for c in rows_c + proj_c + part_c + q_c + hid_c + dn_c + o_c + fin_c + hop_c:
+        c.wait_send()
+
+
+def fused(
+    n_seq, projected, cached, stream, norm_gain, routes, route_gates, gate_weight, up_weight,
+    down_weight,
+):
+    f32, bf16 = jnp.float32, jnp.bfloat16
+    toks = stream.shape[0]
+    span = n_seq * toks
+    heads = cached.shape[0] // GROUP
+    cols = down_weight.shape[1]
+    quarter = gate_weight.shape[1] // GROUP
+    slots = n_seq * CAPACITY
+    vmem = pl.BlockSpec(memory_space=pltpu.VMEM)
+    hbm = pl.BlockSpec(memory_space=pl.ANY)
+    dma = pltpu.SemaphoreType.DMA
+    scratch = [
+        pltpu.VMEM((n_seq, toks, heads * (2 * QK_DIM + V_DIM)), bf16),
+        pltpu.VMEM((GROUP, heads, span, QK_DIM), bf16),
+        pltpu.VMEM((heads, span, QK_DIM), bf16),
+        pltpu.VMEM((heads, span, V_DIM), bf16),
+        pltpu.VMEM(cached.shape, bf16),
+        pltpu.VMEM(gate_weight.shape, bf16),
+        pltpu.VMEM(up_weight.shape, bf16),
+        pltpu.VMEM(down_weight.shape, bf16),
+        pltpu.VMEM((n_seq, CAPACITY, cols), f32),
+        pltpu.VMEM((n_seq, CAPACITY, cols), f32),
+        pltpu.VMEM((GROUP, slots, 2 * quarter), f32),
+        pltpu.VMEM((GROUP, slots, 2 * quarter), f32),
+        pltpu.VMEM((GROUP, slots, quarter), bf16),
+        pltpu.VMEM((n_seq, CAPACITY, cols), f32),
+        pltpu.VMEM((n_seq, CAPACITY, cols), f32),
+        pltpu.VMEM((heads, span, V_DIM), f32),
+        pltpu.VMEM((GROUP, heads, span, V_DIM), bf16),
+        pltpu.VMEM((GROUP, heads, span, V_DIM), bf16),
+        pltpu.VMEM((GROUP, span, 128), f32),
+        pltpu.VMEM((GROUP, span, 128), f32),
+        pltpu.VMEM((n_seq, toks, heads * V_DIM), bf16),
+        pltpu.VMEM((GROUP, n_seq, toks, heads * V_DIM), bf16),
+        dma((3 + GROUP,)),
+        dma,
+        dma((n_seq,)), dma((n_seq,)), dma((n_seq,)), dma((n_seq,)),
+        dma((GROUP,)), dma((GROUP,)), dma((GROUP,)), dma((GROUP,)),
+        dma((GROUP,)), dma((GROUP,)),
+        dma((n_seq,)), dma((n_seq,)),
+        dma((GROUP,)), dma((GROUP,)), dma((GROUP,)), dma((GROUP,)),
+        dma((n_seq,)), dma((n_seq,)), dma((GROUP,)), dma((GROUP,)),
+    ]
+    return pl.pallas_call(
+        functools.partial(one_kernel, n_seq),
+        out_shape=(
+            jax.ShapeDtypeStruct((toks, cached.shape[0] * n_seq * V_DIM), bf16),
+            jax.ShapeDtypeStruct((toks, cols), bf16),
+        ),
+        in_specs=[hbm, hbm, vmem, vmem, vmem, vmem, hbm, hbm, hbm],
+        out_specs=(vmem, vmem),
+        scratch_shapes=scratch,
+        compiler_params=pltpu.CompilerParams(
+            collective_id=0, has_side_effects=True, vmem_limit_bytes=58 * 1024 * 1024
+        ),
+        cost_estimate=pl.CostEstimate(
+            flops=2_000_000_000, bytes_accessed=42_000_000, transcendentals=2_000_000
+        ),
+    )(
+        projected, cached, stream, norm_gain.reshape(1, -1), routes, route_gates,
+        gate_weight, up_weight, down_weight,
+    )
+
+
+def fits(mesh, projected, cached):
+    n_seq, n_fsdp = mesh.shape["seq"], mesh.shape["fsdp"]
+    return (
+        n_seq == WAVE_EXPERTS
+        and n_fsdp == GROUP
+        and projected.shape[0] == 8 * n_seq
+        and cached.shape[0] == 16 * n_seq
+        and cached.shape[2] == 1792 * n_fsdp
+    )
+
+
 def solution(mesh):
     placed = (
         P("seq", None),
@@ -136,10 +490,14 @@
         P("fsdp", "seq"),
         P("seq", "fsdp"),
     )
-    return jax.shard_map(
-        on_device,
-        mesh=mesh,
-        in_specs=placed,
-        out_specs=(P("seq", None), P("seq", "fsdp")),
-        check_vma=False,
-    )
+    outs = (P("seq", None), P("seq", "fsdp"))
+
+    def program(projected, cached, *others):
+        if fits(mesh, projected, cached):
+            body = functools.partial(fused, mesh.shape["seq"])
+        else:
+            body = on_device
+        mapped = jax.shard_map(body, mesh=mesh, in_specs=placed, out_specs=outs, check_vma=False)
+        return mapped(projected, cached, *others)
+
+    return program

time: 236 us -> 47.9 us (0.20)
  matrix products: 69.9 us -> 0 us
  waiting for transfers between devices: 58 us -> 0 us
  Pallas kernels: 0 us -> 44 us
  other arithmetic: 27.9 us -> 0 us
  blocking collectives: 26.4 us -> 0 us
  local copies, waits for them, and re-layouts: 23.6 us -> 3.03 us
  between operations: 14.2 us -> 0.64 us
  starting transfers between devices: 13.5 us -> 0 us
    dot_general x69 -> x0, matrix products: 69.9 us -> none  [the longest x16 31.2 us: head_values(): lax.dot_general(weights_row[:, quarter:], stored[QK_DIM:], contract, pref...]
    pallas_call x0 -> x1, Pallas kernels: none -> 44 us  [fused(): pl.pallas_call(functools.partial(one_kernel, n_seq), out_shape=(jax.Shape...]
    all_to_all x3 -> x0, waiting for transfers between devices: 30.5 us -> none  [the longest x1 17.9 us: on_device(): lax.all_to_all(projected, 'seq', split_axis=1, concat_axis=0, tiled=True)]
    psum x1 -> x0, waiting for transfers between devices: 27.5 us -> none  [on_device(): weighted, key_total = lax.psum((weighted, key_total), 'fsdp')]
    dynamic_update_slice x16 -> x0, other arithmetic: 15.8 us -> none  [on_device(): scores = lax.map(head_scores, (heads_major, cached))]
    squeeze x48 -> x0, local copies, waits for them, and re-layouts: 15.7 us -> none  [the longest x16 15.4 us: on_device(): weighted = lax.map(head_values, (weights_bf, heads_major, cached))]
    all_to_all x1 -> x0, blocking collectives: 13.9 us -> none  [on_device(): lax.all_to_all(outgoing, 'seq', split_axis=0, concat_axis=0, tiled=True)]
    all_to_all x3 -> x0, starting transfers between devices: 13.4 us -> none  [the longest x1 5.51 us: on_device(): lax.all_to_all(partial_value, 'seq', split_axis=0, concat_axis=0, tiled=T...]
  transfers between devices with their start and end apart: 4 -> 0, of which waited for: 4 -> 0; matrix products, arithmetic and copies ran while one was open for 4% -> 0% of each run, Pallas kernels for 0% -> 0%
where the time goes in v2:
time: 47.9 us; the launch traced here: 47.7 us
  Pallas kernels  44 us (92%)
  local copies, waits for them, and re-layouts  3.03 us (6%)
  between operations  0.64 us (1%)
    pallas_call x1, Pallas kernels, fused(): pl.pallas_call(functools.partial(one_kernel, n_seq), out_shape=(jax.Shape...  44 us
    unnamed x2, local copies, waits for them, and re-layouts  3.03 us

profile of v2, /device:TPU:0, one launch (start us, length us, event | category | flops | bytes accessed | tf_op | source)
XLA Modules:
  0.0 47.7 jit_solution(16859413151876948970)
XLA Ops:
  0.6 44.0 %shard_map.104 = (bf16[8,16384]{1,0:T(8,128)(2,1)}, bf16[8,1792]{1,0:T(8,128)(2,1)}) custom-call(bf16[8,65536]{1,0:T(8,128)(2,1)} %proj.1, bf16[16,320,1792]{2,1,0:T(8,128)(2,1)} %cached.1, bf16[8,7168]{1,0:T(8,128)(2,1)} %stream.1, f32[1,7168]{1,0:T(1,128)} %bitcast.1, s32[8,8]{1,0:T(8,128)} %routes.1, f32[8,8]{1,0:T(8,128)} %gates.1, ...), custom_call_target="tpu_custom_call" | custom-call | flops 2000000000 | bytes 42000000 | tf_op jit(solution)/shard_map/pallas_call | solution.py:449
  44.7 1.7 %copy.13 = bf16[8,16384]{1,0:T(8,128)(2,1)} copy(bf16[8,16384]{1,0:T(8,128)(2,1)} %get-tuple-element.4) | data formatting | bytes 524288
  46.3 1.4 %copy.14 = bf16[8,1792]{1,0:T(8,128)(2,1)} copy(bf16[8,1792]{1,0:T(8,128)(2,1)} %get-tuple-element.5) | data formatting | bytes 57344

commit v3 on v2

--- a/solution.py
+++ b/solution.py
@@ -304,7 +304,9 @@
             stats = jnp.where(st_lane == h, top, stats)
             return jnp.where(st_lane == heads + h, total, stats)
 
-        st_buf[x] = lax.fori_loop(0, heads, one_head, jnp.zeros((span, 128), f32))
+        st_buf[x] = lax.fori_loop(
+            0, heads, one_head, jnp.zeros((span, 128), f32), unroll=True
+        )
         if x:
             pair = [
                 remote(o_buf.at[x], o_in.at[x], o_s.at[x], o_r.at[x], s, peers[x]),

time: 47.9 us -> 46.2 us (0.965)
  Pallas kernels: 44 us -> 42.3 us
    pallas_call x1, Pallas kernels: 44 us -> 42.3 us  [fused(): pl.pallas_call(functools.partial(one_kernel, n_seq), out_shape=(jax.Shape...]
where the time goes in v3:
time: 46.2 us; the launch traced here: 46 us
  Pallas kernels  42.3 us (92%)
  local copies, waits for them, and re-layouts  3.03 us (7%)
  between operations  0.64 us (1%)
    pallas_call x1, Pallas kernels, fused(): pl.pallas_call(functools.partial(one_kernel, n_seq), out_shape=(jax.Shape...  42.3 us
    unnamed x2, local copies, waits for them, and re-layouts  3.03 us

profile of v3, /device:TPU:0, one launch (start us, length us, event | category | flops | bytes accessed | tf_op | source)
XLA Modules:
  0.0 46.0 jit_solution(13747879774485055423)
XLA Ops:
  0.6 42.3 %shard_map.104 = (bf16[8,16384]{1,0:T(8,128)(2,1)}, bf16[8,1792]{1,0:T(8,128)(2,1)}) custom-call(bf16[8,65536]{1,0:T(8,128)(2,1)} %proj.1, bf16[16,320,1792]{2,1,0:T(8,128)(2,1)} %cached.1, bf16[8,7168]{1,0:T(8,128)(2,1)} %stream.1, f32[1,7168]{1,0:T(1,128)} %bitcast.1, s32[8,8]{1,0:T(8,128)} %routes.1, f32[8,8]{1,0:T(8,128)} %gates.1, ...), custom_call_target="tpu_custom_call" | custom-call | flops 2000000000 | bytes 42000000 | tf_op jit(solution)/shard_map/pallas_call | solution.py:451
  43.0 1.7 %copy.13 = bf16[8,16384]{1,0:T(8,128)(2,1)} copy(bf16[8,16384]{1,0:T(8,128)(2,1)} %get-tuple-element.4) | data formatting | bytes 524288
  44.6 1.4 %copy.14 = bf16[8,1792]{1,0:T(8,128)(2,1)} copy(bf16[8,1792]{1,0:T(8,128)(2,1)} %get-tuple-element.5) | data formatting | bytes 57344

commit v4 on v3

--- a/solution.py
+++ b/solution.py
@@ -319,6 +319,10 @@
 
     attend(0)
 
+    q_c[0].wait_recv()
+    q_c.append(remote(q_buf.at[f2], q_buf.at[f2], q_s.at[3], q_r.at[3], s, f1))
+    q_c[-1].start()
+
     for c in part_c:
         c.wait_recv()
     both = part[0] + part_in[1] + part_in[2] + part_in[3]
@@ -329,12 +333,10 @@
         hid_c.append(remote(hid.at[f], hid.at[f], hid_s.at[x], hid_r.at[x], s, peers[x]))
         hid_c[-1].start()
 
-    q_c[0].wait_recv()
-    q_c.append(remote(q_buf.at[f2], q_buf.at[f2], q_s.at[3], q_r.at[3], s, f1))
-    q_c[-1].start()
     q_c[1].wait_recv()
     o_c = attend(1)
 
+    o_c += attend(2)
     for c in hid_c:
         c.wait_recv()
     loads[2].wait()
@@ -353,18 +355,8 @@
         dn_c.append(remote(down_out.at[to], down_in.at[s], dn_s.at[k], dn_r.at[k], to, f))
         dn_c[-1].start()
 
-    o_c += attend(2)
     q_c[2].wait_recv()
     o_c += attend(3)
-
-    for c in dn_c:
-        c.wait_recv()
-    mixed = jnp.zeros((toks, cols), f32)
-    for r in range(slots):
-        mixed = mixed + mix[:, r : r + 1] * down_in[
-            r // CAPACITY, r % CAPACITY : r % CAPACITY + 1, :
-        ]
-    routed_out[...] = mixed.astype(bf16)
 
     for c in o_c:
         c.wait_recv()
@@ -386,19 +378,29 @@
         to = lax.rem(s + k, n_seq)
         fin_c.append(remote(fin.at[to], hop.at[f, s], fin_s.at[k], fin_r.at[k], to, f))
         fin_c[-1].start()
+    for c in dn_c:
+        c.wait_recv()
+    mixed = jnp.zeros((toks, cols), f32)
+    for r in range(slots):
+        mixed = mixed + mix[:, r : r + 1] * down_in[
+            r // CAPACITY, r % CAPACITY : r % CAPACITY + 1, :
+        ]
+    routed_out[...] = mixed.astype(bf16)
+
     for c in fin_c:
         c.wait_recv()
     for x in (3, 2, 1):
         hop_c.append(remote(hop.at[f], hop.at[f], hop_s.at[x], hop_r.at[x], s, peers[x]))
         hop_c[-1].start()
-    for c in hop_c:
-        c.wait_recv()
     block = heads * V_DIM
-    for r in range(n_seq):
-        for j in range(GROUP):
-            at = (r * GROUP + j) * block
-            att_out[:, at : at + block] = hop[j, r]
-    for c in rows_c + proj_c + part_c + q_c + hid_c + dn_c + o_c + fin_c + hop_c:
+    hop_c = [None] + hop_c[::-1]
+    for x in range(GROUP):
+        if x:
+            hop_c[x].wait_recv()
+        for r in range(n_seq):
+            at = pl.multiple_of((r * GROUP + peers[x]) * block, 128)
+            att_out[:, pl.ds(at, block)] = hop[peers[x], r]
+    for c in rows_c + proj_c + part_c + q_c + hid_c + dn_c + o_c + fin_c + hop_c[1:]:
         c.wait_send()
 
 

time: 46.2 us -> 45 us (0.974)
  Pallas kernels: 42.3 us -> 41 us
    pallas_call x1, Pallas kernels: 42.3 us -> 41 us  [fused(): pl.pallas_call(functools.partial(one_kernel, n_seq), out_shape=(jax.Shape...]
where the time goes in v4:
time: 45 us; the launch traced here: 44.7 us
  Pallas kernels  41 us (91%)
  local copies, waits for them, and re-layouts  3.03 us (7%)
  between operations  0.64 us (1%)
    pallas_call x1, Pallas kernels, fused(): pl.pallas_call(functools.partial(one_kernel, n_seq), out_shape=(jax.Shape...  41 us
    unnamed x2, local copies, waits for them, and re-layouts  3.03 us

profile of v4, /device:TPU:0, one launch (start us, length us, event | category | flops | bytes accessed | tf_op | source)
XLA Modules:
  0.0 44.7 jit_solution(644725346109376226)
XLA Ops:
  0.6 41.0 %shard_map.104 = (bf16[8,16384]{1,0:T(8,128)(2,1)}, bf16[8,1792]{1,0:T(8,128)(2,1)}) custom-call(bf16[8,65536]{1,0:T(8,128)(2,1)} %proj.1, bf16[16,320,1792]{2,1,0:T(8,128)(2,1)} %cached.1, bf16[8,7168]{1,0:T(8,128)(2,1)} %stream.1, f32[1,7168]{1,0:T(1,128)} %bitcast.1, s32[8,8]{1,0:T(8,128)} %routes.1, f32[8,8]{1,0:T(8,128)} %gates.1, ...), custom_call_target="tpu_custom_call" | custom-call | flops 2000000000 | bytes 42000000 | tf_op jit(solution)/shard_map/pallas_call | solution.py:453
  41.7 1.7 %copy.13 = bf16[8,16384]{1,0:T(8,128)(2,1)} copy(bf16[8,16384]{1,0:T(8,128)(2,1)} %get-tuple-element.4) | data formatting | bytes 524288
  43.3 1.4 %copy.14 = bf16[8,1792]{1,0:T(8,128)(2,1)} copy(bf16[8,1792]{1,0:T(8,128)(2,1)} %get-tuple-element.5) | data formatting | bytes 57344
